TPU v7x, 32 devices: a whole 2x2x4 slice. The times are simulated.
32 devices in a mesh: member: 2 (over y), gx: 16 (over z, x, core).
Axes of the slice: x: 2, y: 2, z: 4, core: 2. Of those that a mesh axis runs over, the one named last changes fastest.
Arguments:
- tracer: float32 [96, 96, 1536], P('member', 'gx'), parts along dimension 0, may hold values from -6 to 6
- frac_x: bfloat16 [96, 96, 1536], P('member', 'gx'), parts along dimension 0, may hold values from 0 to 1
- frac_y: bfloat16 [96, 96, 1536], P('member', 'gx'), parts along dimension 0, may hold values from 0 to 1
- vertical_modes: float32 [48, 48], replicated, may hold values from -0.875 to 0.875
- mode_projection: float32 [48, 48], replicated, may hold values from -0.875 to 0.875
- mode_rates: float32 [48], replicated, may hold values from 1 to 40
Outputs:
- updated: float32 [96, 96, 1536], P('member', 'gx'), parts along dimension 0
There are 2 independent parts, one for each index of `member`. A program takes and returns all parts, laid end to end along the dimension named above; an argument that names none is the same for every part. Nothing has to cross between parts.
All inputs are finite; a program needn't handle non-finite values.
Results may differ from a plain program's by a relative error of at most 0.0003.
Values sent between devices are 32-bit elements; how exact they have to be, the bound alone decides.
A program may use at most 128 MiB of HBM per device.

v0:
```python
import math

import jax
import jax.numpy as jnp
import ml_dtypes
import numpy as np
from jax import lax
from jax.experimental import pallas as pl
from jax.experimental.pallas import tpu as pltpu
from jax.sharding import PartitionSpec as P

HALO = 6


def padded_2(value, sides, width):
    for axis, dim in sides:
        size, length = (lax.axis_size(axis), value.shape[dim])
        up = [(i, (i + 1) % size) for i in range(size)]
        down = [(j, i) for i, j in up]
        last = lax.slice_in_dim(value, length - width, length, axis=dim)
        initial = lax.slice_in_dim(value, 0, width, axis=dim)
        before = lax.ppermute(last, axis, up)
        after = lax.ppermute(initial, axis, down)
        value = jnp.concatenate([before, value, after], axis=dim)
    return value


def lagrange_weights(fraction):
    position = 1.0 - fraction.astype(jnp.float32)
    return (
        -position * (position - 1.0) * (position - 2.0) / 6.0,
        (position + 1.0) * (position - 1.0) * (position - 2.0) / 2.0,
        -(position + 1.0) * position * (position - 2.0) / 2.0,
        (position + 1.0) * position * (position - 1.0) / 6.0,
    )


def drift_classes(levels):
    bounds = []
    for category in range(9):
        first_level = (category * levels + 8) // 9
        last_level = ((category + 1) * levels + 8) // 9
        bounds.append((first_level, last_level, category - 4))
    return bounds


def sweep_columns(values, fraction):
    weights = lagrange_weights(fraction)
    pieces_out = []
    for first_level, last_level, displace in drift_classes(values.shape[0]):
        section = values[first_level:last_level]
        summed = jnp.zeros(section.shape, jnp.float32)
        for stencil in range(4):
            offset = stencil - 2 - displace
            summed = summed + weights[stencil][first_level:last_level] * jnp.roll(
                section, -offset, axis=2
            )
        pieces_out.append(summed)
    return jnp.concatenate(pieces_out, axis=0)


def blend_rows(window, weights, first_level, last_level, displace, anchor, rows_here):
    summed = jnp.zeros((last_level - first_level, rows_here, window.shape[2]), jnp.float32)
    for stencil in range(4):
        offset = anchor + stencil - 2 - displace
        summed = (
            summed
            + weights[stencil][first_level:last_level] * window[:, offset : offset + rows_here]
        )
    return summed


def phase_angles(numbers, places, length):
    phases = jnp.mod(numbers[:, None] * places[None, :], length)
    return phases.astype(jnp.float32) * (2.0 * math.pi / length)


def plain_body(tracer, frac_x, frac_y, vertical_modes, mode_projection, mode_rates):
    levels, rows_here, columns = tracer.shape
    shards = lax.axis_size("gx")
    length_x = rows_here * shards
    modes_x = length_x // 2
    modes_y = columns // 2
    modes_here = modes_y // shards
    interim = sweep_columns(tracer, frac_y)
    weights = lagrange_weights(frac_x)
    classes = drift_classes(levels)
    pieces_out = []
    padded = padded_2(interim, (("gx", 1),), HALO)
    for first_level, last_level, displace in classes:
        pieces_out.append(
            blend_rows(
                padded[first_level:last_level],
                weights,
                first_level,
                last_level,
                displace,
                HALO,
                rows_here,
            )
        )
    advected = jnp.concatenate(pieces_out, axis=0)
    wave_y = jnp.arange(modes_y, dtype=jnp.int32)
    angle_y = phase_angles(wave_y, jnp.arange(columns, dtype=jnp.int32), columns)
    table_y = jnp.stack([jnp.cos(angle_y), -jnp.sin(angle_y)], axis=1).reshape(2 * modes_y, columns)
    flattened = advected.reshape(levels * rows_here, columns)
    coefficients = lax.dot_general(
        table_y, flattened, (((1,), (1,)), ((), ())), precision=lax.Precision.HIGHEST
    )
    coefficients = coefficients.reshape(shards, modes_here, 2, levels * rows_here)
    wave_square = ((2.0 * wave_y.astype(jnp.float32) / columns) ** 2).reshape(shards, modes_here, 1)
    index_x = jnp.arange(modes_x, dtype=jnp.int32)
    wave_x = jnp.where(index_x < modes_x // 2, index_x, index_x - modes_x)
    angle_x = phase_angles(wave_x, jnp.arange(length_x, dtype=jnp.int32), length_x)
    cosine = jnp.cos(angle_x)
    sine = jnp.sin(angle_x)
    forward_x = jnp.stack(
        [jnp.stack([cosine.T, -sine.T], axis=1), jnp.stack([sine.T, cosine.T], axis=1)], axis=1
    )
    forward_x = forward_x.reshape(shards, rows_here, 2, 2, modes_x)
    inverse_x = (
        jnp.stack([jnp.stack([cosine, sine], axis=-1), jnp.stack([-sine, cosine], axis=-1)], axis=0)
        / length_x
    )
    inverse_x = inverse_x.reshape(2, modes_x, shards, rows_here, 2)
    square_x = (2.0 * wave_x.astype(jnp.float32) / length_x) ** 2
    spectral_in = lax.all_to_all(coefficients, "gx", split_axis=0, concat_axis=0, tiled=True)
    square_in = lax.all_to_all(wave_square, "gx", split_axis=0, concat_axis=0, tiled=True)
    item_count = spectral_in.shape[1]
    blocks = spectral_in.reshape(shards, item_count, 2, levels, rows_here)
    spectra = jnp.einsum("nkplc,ncpqm->kqlm", blocks, forward_x, precision=lax.Precision.HIGHEST)
    projected = jnp.einsum(
        "al,kqlm->kqam", mode_projection, spectra, precision=lax.Precision.HIGHEST
    )
    kappa = square_in[0][:, :, None] + square_x[None, None, :]
    factor = 1.0 / (1.0 + mode_rates[None, :, None] * kappa)
    solved = jnp.einsum(
        "la,kqam->kqlm",
        vertical_modes,
        projected * factor[:, None],
        precision=lax.Precision.HIGHEST,
    )
    returned = jnp.einsum("kqlm,qmncp->nkplc", solved, inverse_x, precision=lax.Precision.HIGHEST)
    returned = returned.reshape(shards, item_count, 2, levels * rows_here)
    merged = lax.all_to_all(returned, "gx", split_axis=0, concat_axis=0, tiled=True)
    weights_y = jnp.where(wave_y == 0, 1.0, 2.0).astype(jnp.float32) / columns
    table_back = table_y * jnp.repeat(weights_y, 2)[:, None]
    updated = lax.dot_general(
        merged.reshape(2 * modes_y, levels * rows_here),
        table_back,
        (((0,), (0,)), ((), ())),
        precision=lax.Precision.HIGHEST,
    )
    return updated.reshape(levels, rows_here, columns)


CHUNK = 16
GROUP = 8
VMEM_BYTES = 56 * 1024 * 1024
BF16 = jnp.bfloat16
F32 = jnp.float32


def drift_of(level, levels):
    return (9 * level) // levels - 4


def group_drifts(group, levels):
    first = drift_of(GROUP * group, levels)
    last = drift_of(GROUP * group + GROUP - 1, levels)
    split = next(
        (s for s in range(GROUP) if drift_of(GROUP * group + s, levels) != first), GROUP
    )
    return first, last, split


def halo_groups(levels, rows_here):
    before, after = [], []
    for j in range(rows_here + 3):
        for group in range(levels // GROUP):
            first, last, _ = group_drifts(group, levels)
            if j - 2 - last < 0:
                before.append((j, group))
            if j - 2 - first >= rows_here:
                after.append((j, group))
    return before, after


def split_two(value):
    high = value.astype(BF16)
    return high, (value - high.astype(F32)).astype(BF16)


def dot3(left, right, dims):
    def dot(a, b):
        return lax.dot_general(a, b, (dims, ((), ())), preferred_element_type=F32)

    return dot(left[0], right[0]) + (dot(left[0], right[1]) + dot(left[1], right[0]))


def kernel_weights(fraction):
    p = 1.0 - fraction
    low, lower, upper = p - 1.0, p - 2.0, p + 1.0
    a, b = p * low, upper * lower
    return (
        a * lower * (-1.0 / 6.0),
        b * low * 0.5,
        b * p * (-0.5),
        a * upper * (1.0 / 6.0),
    )


def upper_mask(split, width):
    return lax.broadcasted_iota(jnp.int32, (GROUP, width), 0) >= split


def y_sweep_kernel(tracer, frac, interim, before_out, after_out):
    rows_here, levels, columns = tracer.shape
    for pair in range(levels // (2 * GROUP)):

        @pl.loop(0, rows_here)
        def _(i, pair=pair):
            fractions = frac[i, 2 * GROUP * pair : 2 * GROUP * (pair + 1), :].astype(F32)
            for half in range(2):
                group = 2 * pair + half
                first, last, split = group_drifts(group, levels)
                weights = kernel_weights(fractions[GROUP * half : GROUP * (half + 1)])
                value = tracer[i, GROUP * group : GROUP * (group + 1), :]
                rolled = [
                    pltpu.roll(value, (-(t - 2 - last)) % columns, 1)
                    for t in range(4 + last - first)
                ]
                mask = upper_mask(split, columns)
                total = None
                for tap in range(4):
                    source = rolled[tap]
                    if last != first:
                        source = jnp.where(mask, rolled[tap], rolled[tap + 1])
                    term = weights[tap] * source
                    total = term if total is None else total + term
                interim[i, GROUP * group : GROUP * (group + 1), :] = total

    before, after = halo_groups(levels, rows_here)
    for out, blocks, shift in ((before_out, before, rows_here), (after_out, after, -rows_here)):
        for at, (j, group) in enumerate(blocks):
            first, last, split = group_drifts(group, levels)
            picks = []
            for drift in (first, last):
                row = min(max(j - 2 - drift + shift, 0), rows_here - 1)
                picks.append(interim[row, GROUP * group : GROUP * (group + 1), :])
            out[GROUP * at : GROUP * (at + 1), :] = jnp.where(
                upper_mask(split, picks[0].shape[1]), picks[1], picks[0]
            )


def x_sweep_kernel(interim, frac, before_in, after_in, high_out, low_out):
    rows_here, levels, columns = interim.shape
    before, after = halo_groups(levels, rows_here)
    width = 256

    for pair in range(levels // (2 * GROUP)):

        @pl.loop(0, columns // width)
        def _(step, pair=pair):
            lanes = pl.ds(pl.multiple_of(step * width, width), width)
            windows = []
            for group in (2 * pair, 2 * pair + 1):
                first, last, split = group_drifts(group, levels)
                mask = upper_mask(split, width)
                window = []
                for j in range(rows_here + 3):
                    picks = []
                    for drift in (first, last):
                        row = j - 2 - drift
                        if row < 0:
                            at = GROUP * before.index((j, group))
                            picks.append(before_in[at : at + GROUP, lanes])
                        elif row >= rows_here:
                            at = GROUP * after.index((j, group))
                            picks.append(after_in[at : at + GROUP, lanes])
                        else:
                            at = GROUP * group
                            picks.append(interim[row, at : at + GROUP, lanes])
                    window.append(jnp.where(mask, picks[1], picks[0]))
                windows.append(window)
            for i in range(rows_here):
                at = 2 * GROUP * pair
                weights = kernel_weights(frac[i, at : at + 2 * GROUP, lanes].astype(F32))
                parts = []
                for half in range(2):
                    total = None
                    for tap in range(4):
                        term = (
                            weights[tap][GROUP * half : GROUP * (half + 1)]
                            * windows[half][i + tap]
                        )
                        total = term if total is None else total + term
                    parts.append(total)
                high, low = split_two(jnp.concatenate(parts, axis=0))
                high_out[levels * i + at : levels * i + at + 2 * GROUP, lanes] = high
                low_out[levels * i + at : levels * i + at + 2 * GROUP, lanes] = low


def pack_block(block):
    return jnp.concatenate([block[8 * g : 8 * g + 8] for g in range(4)], axis=1)


def unpack_block(block):
    width = block.shape[1] // 4
    return jnp.concatenate([block[:, width * g : width * (g + 1)] for g in range(4)], axis=0)


def forward_kernel(high, low, table_high, table_low, out):
    shards = out.shape[0]
    rows = table_high.shape[0] // 2
    for part in range(2):
        span = slice(part * rows, (part + 1) * rows)
        result = dot3(
            (table_high[span], table_low[span]), (high[...], low[...]), ((1,), (1,))
        )
        for n in range(shards // 2):
            out[part * (shards // 2) + n] = pack_block(result[32 * n : 32 * n + 32])


def solve_kernel(
    blocks, f_high, f_low, g_high, g_low, twiddle_re, twiddle_im, project, back, kappa, rates, out
):
    shards = blocks.shape[0]
    data = jnp.concatenate([unpack_block(blocks[n]) for n in range(shards)], axis=0)
    plain = ((1,), (0,))
    mixed = dot3((f_high[...], f_low[...]), split_two(data), plain)
    half = mixed.shape[0] // 2
    real, imag = mixed[:half], mixed[half:]
    project_two = split_two(project[...])
    rate = rates[...]
    scale = kappa[:, 3:4]
    out_re = out_im = None
    for part in range(3):
        t_re, t_im = twiddle_re[part], twiddle_im[part]
        turned = (real * t_re - imag * t_im, real * t_im + imag * t_re)
        factor = scale / (1.0 + rate * kappa[:, part : part + 1])
        y_re, y_im = (dot3(split_two(u), project_two, plain) * factor for u in turned)
        a_re = y_re * t_re + y_im * t_im
        a_im = y_im * t_re - y_re * t_im
        out_re = a_re if part == 0 else out_re + a_re
        out_im = a_im if part == 0 else out_im + a_im
    back_two = split_two(back[...])
    solved = jnp.concatenate(
        [dot3(split_two(u), back_two, plain) for u in (out_re, out_im)], axis=0
    )
    result = dot3((g_high[...], g_low[...]), split_two(solved), plain)
    for n in range(shards):
        out[n] = pack_block(result[32 * n : 32 * n + 32])


def inverse_kernel(blocks, table_high, table_low, *rest):
    out = rest[-1]
    data = jnp.concatenate([unpack_block(blocks[n]) for n in range(blocks.shape[0])], axis=0)
    high, low = split_two(data.T)
    width = 512
    for step in range(out.shape[1] // width):
        lanes = slice(step * width, (step + 1) * width)
        value = dot3((high, low), (table_high[:, lanes], table_low[:, lanes]), ((1,), (0,)))
        out[:, lanes] = value if len(rest) == 1 else value + rest[0][:, lanes]


def call(kernel, shapes, flops, args, aliases=None):
    size = sum(math.prod(a.shape) * a.dtype.itemsize for a in (*args, *shapes))
    return pl.pallas_call(
        kernel,
        out_shape=shapes,
        in_specs=[pl.BlockSpec(memory_space=pltpu.VMEM)] * len(args),
        out_specs=[pl.BlockSpec(memory_space=pltpu.VMEM)] * len(shapes),
        input_output_aliases=aliases or {},
        compiler_params=pltpu.CompilerParams(vmem_limit_bytes=VMEM_BYTES),
        cost_estimate=pl.CostEstimate(flops=flops, bytes_accessed=size, transcendentals=0),
    )(*args)


def two_parts(table):
    high = table.astype(ml_dtypes.bfloat16)
    low = (table - high.astype(np.float64)).astype(ml_dtypes.bfloat16)
    return high, low


def y_table(columns, shards, modes_here):
    wave = np.arange(shards * modes_here).reshape(shards, modes_here // CHUNK, CHUNK)
    wave = wave.transpose(1, 0, 2)[..., None]
    angle = (wave * np.arange(columns) % columns) * (2.0 * np.pi / columns)
    table = np.stack([np.cos(angle), -np.sin(angle)], axis=3)
    return two_parts(table.reshape(modes_here // CHUNK, shards * CHUNK * 2, columns))


def x_tables(shards, rows_here, levels):
    n = np.arange(shards)
    angle = (n[:, None] * n[None, :] % shards) * (2.0 * np.pi / shards)
    c, s = np.cos(angle), np.sin(angle)
    forward = np.stack([np.stack([c, s], 1), np.stack([-s, c], 1)], 0)
    eye = np.eye(CHUNK)
    size = 2 * shards * CHUNK
    forward = np.einsum("pmqn,kj->pmknjq", forward, eye).reshape(size, size)
    length_x = shards * rows_here
    modes_x = length_x // 2
    m = np.arange(modes_x)
    wave = np.where(m < modes_x // 2, m, m - modes_x)
    turn = (wave[:, None] * np.arange(rows_here) % length_x) * (2.0 * np.pi / length_x)
    turn = turn.reshape(-1, shards, 1, rows_here, 1)
    shape = (turn.shape[0], shards, CHUNK, rows_here, levels)
    turn = np.broadcast_to(turn, shape).reshape(-1, shards * CHUNK, rows_here * levels)
    square = ((2.0 * wave / length_x) ** 2).reshape(-1, shards).T
    square = np.repeat(square, CHUNK, axis=0).astype(np.float32)
    return (
        two_parts(forward),
        two_parts(np.ascontiguousarray(forward.T)),
        np.cos(turn).astype(np.float32),
        (-np.sin(turn)).astype(np.float32),
        square,
    )


def body(tracer, frac_x, frac_y, vertical_modes, mode_projection, mode_rates):
    levels, rows_here, columns = tracer.shape
    shards = lax.axis_size("gx")
    length_x = rows_here * shards
    modes_y = columns // 2
    modes_here = modes_y // shards
    fits = (
        shards == 16
        and modes_here % CHUNK == 0
        and length_x // 2 == 3 * shards
        and levels % (2 * GROUP) == 0
        and levels <= 48
        and columns % 512 == 0
        and all(
            group_drifts(g, levels)[1] - group_drifts(g, levels)[0] == 1
            for g in range(levels // GROUP)
        )
    )
    if not fits:
        return plain_body(tracer, frac_x, frac_y, vertical_modes, mode_projection, mode_rates)
    lines = rows_here * levels
    chunks = modes_here // CHUNK
    before, after = halo_groups(levels, rows_here)
    interim, to_right, to_left = call(
        y_sweep_kernel,
        [
            jax.ShapeDtypeStruct((rows_here, levels, columns), F32),
            jax.ShapeDtypeStruct((GROUP * len(before), columns), F32),
            jax.ShapeDtypeStruct((GROUP * len(after), columns), F32),
        ],
        40 * lines * columns,
        (jnp.swapaxes(tracer, 0, 1), jnp.swapaxes(frac_y, 0, 1)),
    )
    up = [(i, (i + 1) % shards) for i in range(shards)]
    from_left = lax.ppermute(to_right, "gx", up)
    from_right = lax.ppermute(to_left, "gx", [(j, i) for i, j in up])
    high, low = call(
        x_sweep_kernel,
        [jax.ShapeDtypeStruct((lines, columns), BF16)] * 2,
        40 * lines * columns,
        (interim, jnp.swapaxes(frac_x, 0, 1), from_left, from_right),
    )

    t_high, t_low = y_table(columns, shards, modes_here)
    f_two, g_two, twiddle_re, twiddle_im, square_x = x_tables(shards, rows_here, levels)
    eye = jnp.eye(rows_here, dtype=F32)
    project = jnp.tile(mode_projection.T, (rows_here, rows_here))
    back = (eye[:, None, :, None] * vertical_modes.T[None, :, None, :]).reshape(lines, lines)
    rates = jnp.tile(mode_rates, rows_here)[None, :]
    size = shards * CHUNK * 2
    block = jax.ShapeDtypeStruct((shards, 8, 4 * lines), F32)

    kappas, tables = [], []
    for c in range(chunks):
        wave = lax.axis_index("gx") * modes_here + c * CHUNK + jnp.arange(CHUNK, dtype=jnp.int32)
        square_y = jnp.tile((2.0 * wave.astype(F32) / columns) ** 2, shards)[:, None]
        scale = jnp.where(wave == 0, 1.0, 2.0).astype(F32) / (columns * length_x)
        kappas.append(
            jnp.concatenate([square_x + square_y, jnp.tile(scale, shards)[:, None]], axis=1)
        )
        tables.append((jnp.asarray(t_high[c]), jnp.asarray(t_low[c])))

    def swap(value):
        return lax.all_to_all(value, "gx", split_axis=0, concat_axis=0, tiled=True)

    received = []
    for c in range(chunks):
        (sent,) = call(
            forward_kernel, [block], 6 * size * columns * lines, (high, low, *tables[c])
        )
        received.append(swap(sent))
    returned = []
    for c in range(chunks):
        (solved,) = call(
            solve_kernel,
            [block],
            12 * size * size * lines + 24 * size * lines * lines,
            (
                received[c],
                *map(jnp.asarray, (*f_two, *g_two, twiddle_re, twiddle_im)),
                project,
                back,
                kappas[c],
                rates,
            ),
        )
        returned.append(swap(solved))
    total = ()
    for c in range(chunks):
        total = call(
            inverse_kernel,
            [jax.ShapeDtypeStruct((lines, columns), F32)],
            6 * size * columns * lines,
            (returned[c], *tables[c], *total),
            {3: 0} if c else None,
        )
    return jnp.swapaxes(total[0].reshape(rows_here, levels, columns), 0, 1)


def solution(mesh):
    placed = (
        P("member", "gx", None),
        P("member", "gx", None),
        P("member", "gx", None),
        P(),
        P(),
        P(),
    )
    return jax.shard_map(
        body, mesh=mesh, in_specs=placed, out_specs=P("member", "gx", None), check_vma=False
    )
```

profile of v0, /device:TPU:13, one launch (start us, length us, event | category | flops | bytes accessed | tf_op | source)
XLA Modules:
  0.0 165.1 jit_solution(13872527975231424978)
XLA Ops:
  0.0 6.9 %shard_map.181 = (f32[6,48,1536]{2,1,0:T(8,128)}, f32[128,1536]{1,0:T(8,128)}, f32[96,1536]{1,0:T(8,128)}) custom-call(f32[6,48,1536]{2,1,0:T(8,128)} %bitcast.8, bf16[6,48,1536]{2,1,0:T(8,128)(2,1)} %bitcast.9), custom_call_target="tpu_custom_call" | custom-call | flops 17694720 | bytes 5799936 | tf_op jit(solution)/shard_map/pallas_call | solution.py:369
  6.9 1.8 %collective-permute-start = (f32[128,1536]{1,0:T(8,128)}, f32[128,1536]{1,0:T(8,128)S(1)}, u32[]{:S(2)}, u32[]{:S(2)}) collective-permute-start(f32[128,1536]{1,0:T(8,128)} %get-tuple-element.11), channel_id=1, source_target_pairs={{0,1},{1,2},{2,3},{3,4},{4,5},{5,6},{6,7},{7,8},{8,9},{9,10},{10,1... | collective-permute-start | bytes 2359304 | tf_op jit(solution)/shard_map/ppermute | solution.py:455
  8.7 17.1 %collective-permute-done.1.after_in = f32[96,1536]{1,0:T(8,128)S(1)} collective-permute-done((f32[96,1536]{1,0:T(8,128)}, f32[96,1536]{1,0:T(8,128)S(1)}, u32[]{:S(2)}, u32[]{:S(2)}) %collective-permute-start.1) | collective-permute-done | bytes 589856 | tf_op jit(solution)/shard_map/ppermute | solution.py:456
  25.7 0.8 copy-done.7
  26.8 5.0 %shard_map.182 = (bf16[288,1536]{1,0:T(8,128)(2,1)}, bf16[288,1536]{1,0:T(8,128)(2,1)}) custom-call(f32[6,48,1536]{2,1,0:T(8,128)} %get-tuple-element.10.interim, bf16[6,48,1536]{2,1,0:T(8,128)(2,1)} %bitcast.10, f32[128,1536]{1,0:T(8,128)} %copy-done.3, f32[96,1536]{1,0:T(8,128)} %copy-done.7), custom_call_target="tpu_custom_call" | custom-call | flops 17694720 | bytes 5799936 | tf_op jit(solution)/shard_map/pallas_call | solution.py:369
  31.8 5.9 %shard_map.183 = f32[16,8,1152]{2,1,0:T(8,128)} custom-call(bf16[288,1536]{1,0:T(8,128)(2,1)} %get-tuple-element.13.high, bf16[288,1536]{1,0:T(8,128)(2,1)} %get-tuple-element.14.low, bf16[512,1536]{1,0:T(8,128)(2,1)} %constant.61.clone.table_high, bf16[512,1536]{1,0:T(8,128)(2,1)} %constant.62.clone.table_low), custom_call_target="tpu_custom_call" | custom-call | flops 1358954496 | bytes 5505024 | tf_op jit(solution)/shard_map/pallas_call | solution.py:369
  37.7 5.5 %all-to-all-start = ((f32[16,8,1152]{2,1,0:T(8,128)}), f32[16,8,1152]{2,1,0:T(8,128)S(1)}, u32[]{:S(2)}, u32[]{:S(2)}) async-start(f32[16,8,1152]{2,1,0:T(8,128)} %shard_map.183), calls=%async_computation | async-start | bytes 1179648 | tf_op jit(solution)/shard_map/all_to_all | solution.py:484
  43.2 5.9 %shard_map.185 = f32[16,8,1152]{2,1,0:T(8,128)} custom-call(bf16[288,1536]{1,0:T(8,128)(2,1)} %get-tuple-element.13.high, bf16[288,1536]{1,0:T(8,128)(2,1)} %get-tuple-element.14.low, bf16[512,1536]{1,0:T(8,128)(2,1)} %constant.59.clone.table_high, bf16[512,1536]{1,0:T(8,128)(2,1)} %constant.60.clone.table_low), custom_call_target="tpu_custom_call" | custom-call | flops 1358954496 | bytes 5505024 | tf_op jit(solution)/shard_map/pallas_call | solution.py:369
  49.1 9.6 %all-to-all-done.blocks = f32[16,8,1152]{2,1,0:T(8,128)S(1)} async-done(((f32[16,8,1152]{2,1,0:T(8,128)}), f32[16,8,1152]{2,1,0:T(8,128)S(1)}, u32[]{:S(2)}, u32[]{:S(2)}) %all-to-all-start) | async-done | bytes 589856 | tf_op jit(solution)/shard_map/all_to_all | solution.py:484
  58.7 4.4 %all-to-all-start.2 = ((f32[16,8,1152]{2,1,0:T(8,128)}), f32[16,8,1152]{2,1,0:T(8,128)S(1)}, u32[]{:S(2)}, u32[]{:S(2)}) async-start(f32[16,8,1152]{2,1,0:T(8,128)} %shard_map.185), calls=%async_computation.2 | async-start | bytes 1179648 | tf_op jit(solution)/shard_map/all_to_all | solution.py:484
  63.4 1.1 tile.19.project
  64.5 5.9 %shard_map.187 = f32[16,8,1152]{2,1,0:T(8,128)} custom-call(bf16[288,1536]{1,0:T(8,128)(2,1)} %get-tuple-element.13.high, bf16[288,1536]{1,0:T(8,128)(2,1)} %get-tuple-element.14.low, bf16[512,1536]{1,0:T(8,128)(2,1)} %constant.57.clone.table_high, bf16[512,1536]{1,0:T(8,128)(2,1)} %constant.58.clone.table_low), custom_call_target="tpu_custom_call" | custom-call | flops 1358954496 | bytes 5505024 | tf_op jit(solution)/shard_map/pallas_call | solution.py:369
  70.4 8.3 %all-to-all-done.2.blocks = f32[16,8,1152]{2,1,0:T(8,128)S(1)} async-done(((f32[16,8,1152]{2,1,0:T(8,128)}), f32[16,8,1152]{2,1,0:T(8,128)S(1)}, u32[]{:S(2)}, u32[]{:S(2)}) %all-to-all-start.2) | async-done | bytes 589856 | tf_op jit(solution)/shard_map/all_to_all | solution.py:484
  78.7 4.4 %all-to-all-start.4 = ((f32[16,8,1152]{2,1,0:T(8,128)}), f32[16,8,1152]{2,1,0:T(8,128)S(1)}, u32[]{:S(2)}, u32[]{:S(2)}) async-start(f32[16,8,1152]{2,1,0:T(8,128)} %shard_map.187), calls=%async_computation.4 | async-start | bytes 1179648 | tf_op jit(solution)/shard_map/all_to_all | solution.py:484
  83.3 1.1 mul.31.back
  85.5 0.8 copy.32.kappa
  86.3 9.2 %shard_map.186 = f32[16,8,1152]{2,1,0:T(8,128)} custom-call(f32[16,8,1152]{2,1,0:T(8,128)} %copy-done.6, bf16[512,512]{1,0:T(8,128)(2,1)} %constant.63.clone.f_high, bf16[512,512]{1,0:T(8,128)(2,1)} %constant.64.clone.f_low, bf16[512,512]{1,0:T(8,128)(2,1)} %constant.65.clone.g_high, bf16[512,512]{1,0:T(8,128)(2,1)} %constant.66.clone.g_low, ...), custom_call_target="tpu_custom_call" | custom-call | flops 1925185536 | bytes 5715072 | tf_op jit(solution)/shard_map/pallas_call | solution.py:369
  95.5 3.2 %all-to-all-done.4.blocks = f32[16,8,1152]{2,1,0:T(8,128)S(1)} async-done(((f32[16,8,1152]{2,1,0:T(8,128)}), f32[16,8,1152]{2,1,0:T(8,128)S(1)}, u32[]{:S(2)}, u32[]{:S(2)}) %all-to-all-start.4) | async-done | bytes 589856 | tf_op jit(solution)/shard_map/all_to_all | solution.py:484
  98.7 4.4 %all-to-all-start.3 = ((f32[16,8,1152]{2,1,0:T(8,128)}), f32[16,8,1152]{2,1,0:T(8,128)S(1)}, u32[]{:S(2)}, u32[]{:S(2)}) async-start(f32[16,8,1152]{2,1,0:T(8,128)} %shard_map.186), calls=%async_computation.3 | async-start | bytes 1179648 | tf_op jit(solution)/shard_map/all_to_all | solution.py:484
  103.2 0.8 copy.33.kappa
  104.1 9.2 %shard_map.188 = f32[16,8,1152]{2,1,0:T(8,128)} custom-call(f32[16,8,1152]{2,1,0:T(8,128)} %copy-done.5, bf16[512,512]{1,0:T(8,128)(2,1)} %constant.63.clone.f_high, bf16[512,512]{1,0:T(8,128)(2,1)} %constant.64.clone.f_low, bf16[512,512]{1,0:T(8,128)(2,1)} %constant.65.clone.g_high, bf16[512,512]{1,0:T(8,128)(2,1)} %constant.66.clone.g_low, ...), custom_call_target="tpu_custom_call" | custom-call | flops 1925185536 | bytes 5715072 | tf_op jit(solution)/shard_map/pallas_call | solution.py:369
  113.2 5.5 %all-to-all-done.3.blocks = f32[16,8,1152]{2,1,0:T(8,128)S(1)} async-done(((f32[16,8,1152]{2,1,0:T(8,128)}), f32[16,8,1152]{2,1,0:T(8,128)S(1)}, u32[]{:S(2)}, u32[]{:S(2)}) %all-to-all-start.3) | async-done | bytes 589856 | tf_op jit(solution)/shard_map/all_to_all | solution.py:484
  118.7 4.4 %all-to-all-start.5 = ((f32[16,8,1152]{2,1,0:T(8,128)}), f32[16,8,1152]{2,1,0:T(8,128)S(1)}, u32[]{:S(2)}, u32[]{:S(2)}) async-start(f32[16,8,1152]{2,1,0:T(8,128)} %shard_map.188), calls=%async_computation.5 | async-start | bytes 1179648 | tf_op jit(solution)/shard_map/all_to_all | solution.py:484
  123.2 0.8 copy.31.kappa
  124.0 9.2 %shard_map.184 = f32[16,8,1152]{2,1,0:T(8,128)} custom-call(f32[16,8,1152]{2,1,0:T(8,128)} %copy-done.4, bf16[512,512]{1,0:T(8,128)(2,1)} %constant.63.clone.f_high, bf16[512,512]{1,0:T(8,128)(2,1)} %constant.64.clone.f_low, bf16[512,512]{1,0:T(8,128)(2,1)} %constant.65.clone.g_high, bf16[512,512]{1,0:T(8,128)(2,1)} %constant.66.clone.g_low, ...), custom_call_target="tpu_custom_call" | custom-call | flops 1925185536 | bytes 5715072 | tf_op jit(solution)/shard_map/pallas_call | solution.py:369
  133.2 5.4 %all-to-all-done.5.blocks = f32[16,8,1152]{2,1,0:T(8,128)S(1)} async-done(((f32[16,8,1152]{2,1,0:T(8,128)}), f32[16,8,1152]{2,1,0:T(8,128)S(1)}, u32[]{:S(2)}, u32[]{:S(2)}) %all-to-all-start.5) | async-done | bytes 589856 | tf_op jit(solution)/shard_map/all_to_all | solution.py:484
  138.7 4.4 %all-to-all-start.1 = ((f32[16,8,1152]{2,1,0:T(8,128)}), f32[16,8,1152]{2,1,0:T(8,128)S(1)}, u32[]{:S(2)}, u32[]{:S(2)}) async-start(f32[16,8,1152]{2,1,0:T(8,128)} %shard_map.184), calls=%async_computation.1 | async-start | bytes 1179648 | tf_op jit(solution)/shard_map/all_to_all | solution.py:484
  143.1 5.1 %shard_map.189.rest_0_ = f32[288,1536]{1,0:T(8,128)} custom-call(f32[16,8,1152]{2,1,0:T(8,128)} %copy-done.2, bf16[512,1536]{1,0:T(8,128)(2,1)} %constant.57.clone.table_high, bf16[512,1536]{1,0:T(8,128)(2,1)} %constant.58.clone.table_low), custom_call_target="tpu_custom_call" | custom-call | flops 1358954496 | bytes 5505024 | tf_op jit(solution)/shard_map/pallas_call | solution.py:369
  148.2 5.6 %shard_map.190.rest_0_ = f32[288,1536]{1,0:T(8,128)} custom-call(f32[16,8,1152]{2,1,0:T(8,128)} %copy-done, bf16[512,1536]{1,0:T(8,128)(2,1)} %constant.59.clone.table_high, bf16[512,1536]{1,0:T(8,128)(2,1)} %constant.60.clone.table_low, f32[288,1536]{1,0:T(8,128)} %shard_map.189.rest_0_), custom_call_target="tpu_custom_call", output_to_operand_aliasing={{}: (3, {})} | custom-call | flops 1358954496 | bytes 7274496 | tf_op jit(solution)/shard_map/pallas_call | solution.py:369
  153.8 4.8 %all-to-all-done.1.blocks = f32[16,8,1152]{2,1,0:T(8,128)S(1)} async-done(((f32[16,8,1152]{2,1,0:T(8,128)}), f32[16,8,1152]{2,1,0:T(8,128)S(1)}, u32[]{:S(2)}, u32[]{:S(2)}) %all-to-all-start.1) | async-done | bytes 589856 | tf_op jit(solution)/shard_map/all_to_all | solution.py:484
  158.6 0.8 copy-done.1
  159.4 5.6 %shard_map.191 = f32[288,1536]{1,0:T(8,128)} custom-call(f32[16,8,1152]{2,1,0:T(8,128)} %copy-done.1, bf16[512,1536]{1,0:T(8,128)(2,1)} %constant.61.clone.table_high, bf16[512,1536]{1,0:T(8,128)(2,1)} %constant.62.clone.table_low, f32[288,1536]{1,0:T(8,128)} %shard_map.190.rest_0_), custom_call_target="tpu_custom_call", output_to_operand_aliasing={{}: (3, {})} | custom-call | flops 1358954496 | bytes 7274496 | tf_op jit(solution)/shard_map/pallas_call | solution.py:369
  (50 shorter events, 1.9 us)
Async XLA Ops:
  6.9 18.8 %collective-permute-start = (f32[128,1536]{1,0:T(8,128)}, f32[128,1536]{1,0:T(8,128)S(1)}, u32[]{:S(2)}, u32[]{:S(2)}) collective-permute-start(f32[128,1536]{1,0:T(8,128)} %get-tuple-element.11), channel_id=1, source_target_pairs={{0,1},{1,2},{2,3},{3,4},{4,5},{5,6},{6,7},{7,8},{8,9},{9,10},{10,1... | collective-permute-start | bytes 2359304 | tf_op jit(solution)/shard_map/ppermute | solution.py:455
  8.6 17.1 %collective-permute-start.1 = (f32[96,1536]{1,0:T(8,128)}, f32[96,1536]{1,0:T(8,128)S(1)}, u32[]{:S(2)}, u32[]{:S(2)}) collective-permute-start(f32[96,1536]{1,0:T(8,128)} %get-tuple-element.12), channel_id=1, source_target_pairs={{1,0},{2,1},{3,2},{4,3},{5,4},{6,5},{7,6},{8,7},{9,8},{10,9},{11,1... | collective-permute-start | bytes 1769480 | tf_op jit(solution)/shard_map/ppermute | solution.py:456
  25.7 0.8 copy-start.7
  25.7 1.1 copy-start.3
  37.7 21.0 %all-to-all-start = ((f32[16,8,1152]{2,1,0:T(8,128)}), f32[16,8,1152]{2,1,0:T(8,128)S(1)}, u32[]{:S(2)}, u32[]{:S(2)}) async-start(f32[16,8,1152]{2,1,0:T(8,128)} %shard_map.183), calls=%async_computation | async-start | bytes 1179648 | tf_op jit(solution)/shard_map/all_to_all | solution.py:484
  43.2 20.0 %copy-start.8 = (f32[48,48]{1,0:T(8,128)S(1)}, f32[48,48]{1,0:T(8,128)}, u32[]{:S(2)}) copy-start(f32[48,48]{1,0:T(8,128)} %param.23) | copy-start | bytes 27652
  58.7 5.7 %copy-start.4 = (f32[16,8,1152]{2,1,0:T(8,128)}, f32[16,8,1152]{2,1,0:T(8,128)S(1)}, u32[]{:S(2)}) copy-start(f32[16,8,1152]{2,1,0:T(8,128)S(1)} %all-to-all-done.blocks) | copy-start | bytes 1769476
  58.7 20.0 %all-to-all-start.2 = ((f32[16,8,1152]{2,1,0:T(8,128)}), f32[16,8,1152]{2,1,0:T(8,128)S(1)}, u32[]{:S(2)}, u32[]{:S(2)}) async-start(f32[16,8,1152]{2,1,0:T(8,128)} %shard_map.185), calls=%async_computation.2 | async-start | bytes 1179648 | tf_op jit(solution)/shard_map/all_to_all | solution.py:484
  63.2 1.2 copy-start.9
  78.7 5.7 %copy-start.6 = (f32[16,8,1152]{2,1,0:T(8,128)}, f32[16,8,1152]{2,1,0:T(8,128)S(1)}, u32[]{:S(2)}) copy-start(f32[16,8,1152]{2,1,0:T(8,128)S(1)} %all-to-all-done.2.blocks) | copy-start | bytes 1769476
  78.7 20.0 %all-to-all-start.4 = ((f32[16,8,1152]{2,1,0:T(8,128)}), f32[16,8,1152]{2,1,0:T(8,128)S(1)}, u32[]{:S(2)}, u32[]{:S(2)}) async-start(f32[16,8,1152]{2,1,0:T(8,128)} %shard_map.187), calls=%async_computation.4 | async-start | bytes 1179648 | tf_op jit(solution)/shard_map/all_to_all | solution.py:484
  83.2 1.5 copy-start.11
  83.2 2.3 %copy-start.10 = (f32[256,3]{0,1:T(4,128)S(1)}, f32[256,3]{0,1:T(4,128)}, u32[]{:S(2)}) copy-start(f32[256,3]{0,1:T(4,128)} %constant.56.clone) | copy-start | bytes 9220
  98.7 5.4 %copy-start.5 = (f32[16,8,1152]{2,1,0:T(8,128)}, f32[16,8,1152]{2,1,0:T(8,128)S(1)}, u32[]{:S(2)}) copy-start(f32[16,8,1152]{2,1,0:T(8,128)S(1)} %all-to-all-done.4.blocks) | copy-start | bytes 1769476
  98.7 20.0 %all-to-all-start.3 = ((f32[16,8,1152]{2,1,0:T(8,128)}), f32[16,8,1152]{2,1,0:T(8,128)S(1)}, u32[]{:S(2)}, u32[]{:S(2)}) async-start(f32[16,8,1152]{2,1,0:T(8,128)} %shard_map.186), calls=%async_computation.3 | async-start | bytes 1179648 | tf_op jit(solution)/shard_map/all_to_all | solution.py:484
  118.7 14.5 %copy-start = (f32[16,8,1152]{2,1,0:T(8,128)}, f32[16,8,1152]{2,1,0:T(8,128)S(1)}, u32[]{:S(2)}) copy-start(f32[16,8,1152]{2,1,0:T(8,128)S(1)} %all-to-all-done.3.blocks) | copy-start | bytes 1769476
  118.7 20.0 %all-to-all-start.5 = ((f32[16,8,1152]{2,1,0:T(8,128)}), f32[16,8,1152]{2,1,0:T(8,128)S(1)}, u32[]{:S(2)}, u32[]{:S(2)}) async-start(f32[16,8,1152]{2,1,0:T(8,128)} %shard_map.188), calls=%async_computation.5 | async-start | bytes 1179648 | tf_op jit(solution)/shard_map/all_to_all | solution.py:484
  138.7 4.5 %copy-start.2 = (f32[16,8,1152]{2,1,0:T(8,128)}, f32[16,8,1152]{2,1,0:T(8,128)S(1)}, u32[]{:S(2)}) copy-start(f32[16,8,1152]{2,1,0:T(8,128)S(1)} %all-to-all-done.5.blocks) | copy-start | bytes 1769476
  138.7 20.0 %all-to-all-start.1 = ((f32[16,8,1152]{2,1,0:T(8,128)}), f32[16,8,1152]{2,1,0:T(8,128)S(1)}, u32[]{:S(2)}, u32[]{:S(2)}) async-start(f32[16,8,1152]{2,1,0:T(8,128)} %shard_map.184), calls=%async_computation.1 | async-start | bytes 1179648 | tf_op jit(solution)/shard_map/all_to_all | solution.py:484
  158.6 0.8 copy-start.1
where the time goes:
time: 167 us; the launch traced here: 165 us
  Pallas kernels  73.5 us (44%)
  waiting for transfers between devices  53.9 us (32%)
  starting transfers between devices  29.5 us (18%)
  local copies, waits for them, and re-layouts  7.82 us (5%)
    pallas_call x11, Pallas kernels, call(): pl.pallas_call(kernel, out_shape=shapes, in_specs=[pl.BlockSpec(memory_sp...  73.5 us
    all_to_all x6, waiting for transfers between devices, swap(): return lax.all_to_all(value, 'gx', split_axis=0, concat_axis=0, tiled=True)  36.9 us
    all_to_all x6, starting transfers between devices, swap(): return lax.all_to_all(value, 'gx', split_axis=0, concat_axis=0, tiled=True)  27.8 us
    ppermute x1, waiting for transfers between devices, body(): from_right = lax.ppermute(to_left, 'gx', [(j, i) for i, j in up])  17.1 us
  transfers between devices with their start and end apart: 8, of which 7 were waited for; matrix products, arithmetic and copies ran while one was open for 4% of the time, Pallas kernels for 30%

commit v1 on v0

--- a/solution.py
+++ b/solution.py
@@ -154,8 +154,10 @@
     return updated.reshape(levels, rows_here, columns)
 
 
-CHUNK = 16
+CHUNK = 24
 GROUP = 8
+SPAN = 2 * CHUNK
+PIECES = SPAN // 8
 VMEM_BYTES = 56 * 1024 * 1024
 BF16 = jnp.bfloat16
 F32 = jnp.float32
@@ -302,12 +304,12 @@
 
 
 def pack_block(block):
-    return jnp.concatenate([block[8 * g : 8 * g + 8] for g in range(4)], axis=1)
+    return jnp.concatenate([block[8 * g : 8 * g + 8] for g in range(PIECES)], axis=1)
 
 
 def unpack_block(block):
-    width = block.shape[1] // 4
-    return jnp.concatenate([block[:, width * g : width * (g + 1)] for g in range(4)], axis=0)
+    width = block.shape[1] // PIECES
+    return jnp.concatenate([block[:, width * g : width * (g + 1)] for g in range(PIECES)], axis=0)
 
 
 def forward_kernel(high, low, table_high, table_low, out):
@@ -319,7 +321,7 @@
             (table_high[span], table_low[span]), (high[...], low[...]), ((1,), (1,))
         )
         for n in range(shards // 2):
-            out[part * (shards // 2) + n] = pack_block(result[32 * n : 32 * n + 32])
+            out[part * (shards // 2) + n] = pack_block(result[SPAN * n : SPAN * n + SPAN])
 
 
 def solve_kernel(
@@ -350,7 +352,7 @@
     )
     result = dot3((g_high[...], g_low[...]), split_two(solved), plain)
     for n in range(shards):
-        out[n] = pack_block(result[32 * n : 32 * n + 32])
+        out[n] = pack_block(result[SPAN * n : SPAN * n + SPAN])
 
 
 def inverse_kernel(blocks, table_high, table_low, *rest):
@@ -468,7 +470,7 @@
     back = (eye[:, None, :, None] * vertical_modes.T[None, :, None, :]).reshape(lines, lines)
     rates = jnp.tile(mode_rates, rows_here)[None, :]
     size = shards * CHUNK * 2
-    block = jax.ShapeDtypeStruct((shards, 8, 4 * lines), F32)
+    block = jax.ShapeDtypeStruct((shards, 8, PIECES * lines), F32)
 
     kappas, tables = [], []
     for c in range(chunks):

time: 167 us -> 157 us (0.940)
  starting transfers between devices: 29.5 us -> 21.7 us
  Pallas kernels: 73.5 us -> 68.8 us
  waiting for transfers between devices: 53.9 us -> 58.2 us
    all_to_all x6 -> x4, starting transfers between devices: 27.8 us -> 19.9 us  [swap(): return lax.all_to_all(value, 'gx', split_axis=0, concat_axis=0, tiled=True)]
    pallas_call x11 -> x8, Pallas kernels: 73.5 us -> 68.8 us  [call(): pl.pallas_call(kernel, out_shape=shapes, in_specs=[pl.BlockSpec(memory_sp...]
    all_to_all x6 -> x4, waiting for transfers between devices: 36.9 us -> 41.1 us  [swap(): return lax.all_to_all(value, 'gx', split_axis=0, concat_axis=0, tiled=True)]
  transfers between devices with their start and end apart: 8 -> 6, of which waited for: 7 -> 5; matrix products, arithmetic and copies ran while one was open for 4% -> 3% of each run, Pallas kernels for 30% -> 27%
where the time goes in v1:
time: 157 us; the launch traced here: 156 us
  Pallas kernels  68.8 us (44%)
  waiting for transfers between devices  58.2 us (37%)
  starting transfers between devices  21.7 us (14%)
  local copies, waits for them, and re-layouts  7.06 us (4%)
    pallas_call x8, Pallas kernels, call(): pl.pallas_call(kernel, out_shape=shapes, in_specs=[pl.BlockSpec(memory_sp...  68.8 us
    all_to_all x4, waiting for transfers between devices, swap(): return lax.all_to_all(value, 'gx', split_axis=0, concat_axis=0, tiled=True)  41.1 us
    all_to_all x4, starting transfers between devices, swap(): return lax.all_to_all(value, 'gx', split_axis=0, concat_axis=0, tiled=True)  19.9 us
    ppermute x1, waiting for transfers between devices, body(): from_right = lax.ppermute(to_left, 'gx', [(j, i) for i, j in up])  17.1 us
  transfers between devices with their start and end apart: 6, of which 5 were waited for; matrix products, arithmetic and copies ran while one was open for 3% of the time, Pallas kernels for 27%

profile of v1, /device:TPU:13, one launch (start us, length us, event | category | flops | bytes accessed | tf_op | source)
XLA Modules:
  0.0 156.1 jit_solution(2412029702074591515)
XLA Ops:
  0.0 6.8 %shard_map.163 = (f32[6,48,1536]{2,1,0:T(8,128)}, f32[128,1536]{1,0:T(8,128)}, f32[96,1536]{1,0:T(8,128)}) custom-call(f32[6,48,1536]{2,1,0:T(8,128)} %bitcast.8, bf16[6,48,1536]{2,1,0:T(8,128)(2,1)} %bitcast.9), custom_call_target="tpu_custom_call" | custom-call | flops 17694720 | bytes 5799936 | tf_op jit(solution)/shard_map/pallas_call | solution.py:371
  6.8 1.8 %collective-permute-start = (f32[128,1536]{1,0:T(8,128)}, f32[128,1536]{1,0:T(8,128)S(1)}, u32[]{:S(2)}, u32[]{:S(2)}) collective-permute-start(f32[128,1536]{1,0:T(8,128)} %get-tuple-element.11), channel_id=1, source_target_pairs={{0,1},{1,2},{2,3},{3,4},{4,5},{5,6},{6,7},{7,8},{8,9},{9,10},{10,1... | collective-permute-start | bytes 2359304 | tf_op jit(solution)/shard_map/ppermute | solution.py:457
  8.6 17.1 %collective-permute-done.1.after_in = f32[96,1536]{1,0:T(8,128)S(1)} collective-permute-done((f32[96,1536]{1,0:T(8,128)}, f32[96,1536]{1,0:T(8,128)S(1)}, u32[]{:S(2)}, u32[]{:S(2)}) %collective-permute-start.1) | collective-permute-done | bytes 589856 | tf_op jit(solution)/shard_map/ppermute | solution.py:458
  25.7 0.8 copy-done.5
  26.5 0.3 copy-done.4
  26.8 5.0 %shard_map.164 = (bf16[288,1536]{1,0:T(8,128)(2,1)}, bf16[288,1536]{1,0:T(8,128)(2,1)}) custom-call(f32[6,48,1536]{2,1,0:T(8,128)} %get-tuple-element.10.interim, bf16[6,48,1536]{2,1,0:T(8,128)(2,1)} %bitcast.10, f32[128,1536]{1,0:T(8,128)} %copy-done.4, f32[96,1536]{1,0:T(8,128)} %copy-done.5), custom_call_target="tpu_custom_call" | custom-call | flops 17694720 | bytes 5799936 | tf_op jit(solution)/shard_map/pallas_call | solution.py:371
  31.8 7.7 %shard_map.167 = f32[16,8,1728]{2,1,0:T(8,128)} custom-call(bf16[288,1536]{1,0:T(8,128)(2,1)} %get-tuple-element.13.high, bf16[288,1536]{1,0:T(8,128)(2,1)} %get-tuple-element.14.low, bf16[768,1536]{1,0:T(8,128)(2,1)} %constant.48.clone.table_high, bf16[768,1536]{1,0:T(8,128)(2,1)} %constant.49.clone.table_low), custom_call_target="tpu_custom_call" | custom-call | flops 2038431744 | bytes 7372800 | tf_op jit(solution)/shard_map/pallas_call | solution.py:371
  39.5 5.5 %all-to-all-start.2 = ((f32[16,8,1728]{2,1,0:T(8,128)}), f32[16,8,1728]{2,1,0:T(8,128)S(1)}, u32[]{:S(2)}, u32[]{:S(2)}) async-start(f32[16,8,1728]{2,1,0:T(8,128)} %shard_map.167), calls=%async_computation.2 | async-start | bytes 1835008 | tf_op jit(solution)/shard_map/all_to_all | solution.py:486
  45.0 7.7 %shard_map.165 = f32[16,8,1728]{2,1,0:T(8,128)} custom-call(bf16[288,1536]{1,0:T(8,128)(2,1)} %get-tuple-element.13.high, bf16[288,1536]{1,0:T(8,128)(2,1)} %get-tuple-element.14.low, bf16[768,1536]{1,0:T(8,128)(2,1)} %constant.50.clone.table_high, bf16[768,1536]{1,0:T(8,128)(2,1)} %constant.51.clone.table_low), custom_call_target="tpu_custom_call" | custom-call | flops 2038431744 | bytes 7372800 | tf_op jit(solution)/shard_map/pallas_call | solution.py:371
  52.7 14.5 %all-to-all-done.2.blocks = f32[16,8,1728]{2,1,0:T(8,128)S(1)} async-done(((f32[16,8,1728]{2,1,0:T(8,128)}), f32[16,8,1728]{2,1,0:T(8,128)S(1)}, u32[]{:S(2)}, u32[]{:S(2)}) %all-to-all-start.2) | async-done | bytes 884768 | tf_op jit(solution)/shard_map/all_to_all | solution.py:486
  67.2 4.8 %all-to-all-start = ((f32[16,8,1728]{2,1,0:T(8,128)}), f32[16,8,1728]{2,1,0:T(8,128)S(1)}, u32[]{:S(2)}, u32[]{:S(2)}) async-start(f32[16,8,1728]{2,1,0:T(8,128)} %shard_map.165), calls=%async_computation | async-start | bytes 1835008 | tf_op jit(solution)/shard_map/all_to_all | solution.py:486
  72.1 0.1 tile.14
  72.2 1.1 tile.15.project
  73.4 0.1 broadcast_multiply_fusion
  73.5 1.0 mul.28.back
  74.6 0.1 add.57
  74.7 0.1 add.52
  74.8 0.7 broadcast_in_dim_tile.12.rates
  75.5 0.1 broadcast_in_dim_tile.13
  75.6 0.8 copy.28.kappa
  76.4 14.0 %shard_map.168 = f32[16,8,1728]{2,1,0:T(8,128)} custom-call(f32[16,8,1728]{2,1,0:T(8,128)} %copy-done.2, bf16[768,768]{1,0:T(8,128)(2,1)} %constant.52.clone.f_high, bf16[768,768]{1,0:T(8,128)(2,1)} %constant.53.clone.f_low, bf16[768,768]{1,0:T(8,128)(2,1)} %constant.54.clone.g_high, bf16[768,768]{1,0:T(8,128)(2,1)} %constant.55.clone.g_low, ...), custom_call_target="tpu_custom_call" | custom-call | flops 3567255552 | bytes 9813120 | tf_op jit(solution)/shard_map/pallas_call | solution.py:371
  90.5 3.7 %all-to-all-done.blocks = f32[16,8,1728]{2,1,0:T(8,128)S(1)} async-done(((f32[16,8,1728]{2,1,0:T(8,128)}), f32[16,8,1728]{2,1,0:T(8,128)S(1)}, u32[]{:S(2)}, u32[]{:S(2)}) %all-to-all-start) | async-done | bytes 884768 | tf_op jit(solution)/shard_map/all_to_all | solution.py:486
  94.2 4.8 %all-to-all-start.3 = ((f32[16,8,1728]{2,1,0:T(8,128)}), f32[16,8,1728]{2,1,0:T(8,128)S(1)}, u32[]{:S(2)}, u32[]{:S(2)}) async-start(f32[16,8,1728]{2,1,0:T(8,128)} %shard_map.168), calls=%async_computation.3 | async-start | bytes 1835008 | tf_op jit(solution)/shard_map/all_to_all | solution.py:486
  99.0 0.1 broadcast_in_dim_tile.11
  99.1 0.8 copy.27.kappa
  100.0 14.1 %shard_map.166 = f32[16,8,1728]{2,1,0:T(8,128)} custom-call(f32[16,8,1728]{2,1,0:T(8,128)} %copy-done.1, bf16[768,768]{1,0:T(8,128)(2,1)} %constant.52.clone.f_high, bf16[768,768]{1,0:T(8,128)(2,1)} %constant.53.clone.f_low, bf16[768,768]{1,0:T(8,128)(2,1)} %constant.54.clone.g_high, bf16[768,768]{1,0:T(8,128)(2,1)} %constant.55.clone.g_low, ...), custom_call_target="tpu_custom_call" | custom-call | flops 3567255552 | bytes 9813120 | tf_op jit(solution)/shard_map/pallas_call | solution.py:371
  114.0 7.2 %all-to-all-done.3.blocks = f32[16,8,1728]{2,1,0:T(8,128)S(1)} async-done(((f32[16,8,1728]{2,1,0:T(8,128)}), f32[16,8,1728]{2,1,0:T(8,128)S(1)}, u32[]{:S(2)}, u32[]{:S(2)}) %all-to-all-start.3) | async-done | bytes 884768 | tf_op jit(solution)/shard_map/all_to_all | solution.py:486
  121.2 4.8 %all-to-all-start.1 = ((f32[16,8,1728]{2,1,0:T(8,128)}), f32[16,8,1728]{2,1,0:T(8,128)S(1)}, u32[]{:S(2)}, u32[]{:S(2)}) async-start(f32[16,8,1728]{2,1,0:T(8,128)} %shard_map.166), calls=%async_computation.1 | async-start | bytes 1835008 | tf_op jit(solution)/shard_map/all_to_all | solution.py:486
  126.0 6.5 %shard_map.169.rest_0_ = f32[288,1536]{1,0:T(8,128)} custom-call(f32[16,8,1728]{2,1,0:T(8,128)} %copy-done.3, bf16[768,1536]{1,0:T(8,128)(2,1)} %constant.48.clone.table_high, bf16[768,1536]{1,0:T(8,128)(2,1)} %constant.49.clone.table_low), custom_call_target="tpu_custom_call" | custom-call | flops 2038431744 | bytes 7372800 | tf_op jit(solution)/shard_map/pallas_call | solution.py:371
  132.5 15.7 %all-to-all-done.1.blocks = f32[16,8,1728]{2,1,0:T(8,128)S(1)} async-done(((f32[16,8,1728]{2,1,0:T(8,128)}), f32[16,8,1728]{2,1,0:T(8,128)S(1)}, u32[]{:S(2)}, u32[]{:S(2)}) %all-to-all-start.1) | async-done | bytes 884768 | tf_op jit(solution)/shard_map/all_to_all | solution.py:486
  148.2 0.9 copy-done
  149.1 7.0 %shard_map.170 = f32[288,1536]{1,0:T(8,128)} custom-call(f32[16,8,1728]{2,1,0:T(8,128)} %copy-done, bf16[768,1536]{1,0:T(8,128)(2,1)} %constant.50.clone.table_high, bf16[768,1536]{1,0:T(8,128)(2,1)} %constant.51.clone.table_low, f32[288,1536]{1,0:T(8,128)} %shard_map.169.rest_0_), custom_call_target="tpu_custom_call", output_to_operand_aliasing={{}: (3, {})} | custom-call | flops 2038431744 | bytes 9142272 | tf_op jit(solution)/shard_map/pallas_call | solution.py:371
  (32 shorter events, 0.2 us)
Async XLA Ops:
  6.8 18.8 %collective-permute-start = (f32[128,1536]{1,0:T(8,128)}, f32[128,1536]{1,0:T(8,128)S(1)}, u32[]{:S(2)}, u32[]{:S(2)}) collective-permute-start(f32[128,1536]{1,0:T(8,128)} %get-tuple-element.11), channel_id=1, source_target_pairs={{0,1},{1,2},{2,3},{3,4},{4,5},{5,6},{6,7},{7,8},{8,9},{9,10},{10,1... | collective-permute-start | bytes 2359304 | tf_op jit(solution)/shard_map/ppermute | solution.py:457
  8.6 17.1 %collective-permute-start.1 = (f32[96,1536]{1,0:T(8,128)}, f32[96,1536]{1,0:T(8,128)S(1)}, u32[]{:S(2)}, u32[]{:S(2)}) collective-permute-start(f32[96,1536]{1,0:T(8,128)} %get-tuple-element.12), channel_id=1, source_target_pairs={{1,0},{2,1},{3,2},{4,3},{5,4},{6,5},{7,6},{8,7},{9,8},{10,9},{11,1... | collective-permute-start | bytes 1769480 | tf_op jit(solution)/shard_map/ppermute | solution.py:458
  25.7 0.8 copy-start.5
  25.7 1.1 copy-start.4
  39.5 27.7 %all-to-all-start.2 = ((f32[16,8,1728]{2,1,0:T(8,128)}), f32[16,8,1728]{2,1,0:T(8,128)S(1)}, u32[]{:S(2)}, u32[]{:S(2)}) async-start(f32[16,8,1728]{2,1,0:T(8,128)} %shard_map.167), calls=%async_computation.2 | async-start | bytes 1835008 | tf_op jit(solution)/shard_map/all_to_all | solution.py:486
  52.7 19.3 %copy-start.6 = (f32[48,48]{1,0:T(8,128)S(1)}, f32[48,48]{1,0:T(8,128)}, u32[]{:S(2)}) copy-start(f32[48,48]{1,0:T(8,128)} %param.21) | copy-start | bytes 27652
  67.2 6.1 %copy-start.2 = (f32[16,8,1728]{2,1,0:T(8,128)}, f32[16,8,1728]{2,1,0:T(8,128)S(1)}, u32[]{:S(2)}) copy-start(f32[16,8,1728]{2,1,0:T(8,128)S(1)} %all-to-all-done.2.blocks) | copy-start | bytes 2654212
  67.2 27.0 %all-to-all-start = ((f32[16,8,1728]{2,1,0:T(8,128)}), f32[16,8,1728]{2,1,0:T(8,128)S(1)}, u32[]{:S(2)}, u32[]{:S(2)}) async-start(f32[16,8,1728]{2,1,0:T(8,128)} %shard_map.165), calls=%async_computation | async-start | bytes 1835008 | tf_op jit(solution)/shard_map/all_to_all | solution.py:486
  72.0 1.3 copy-start.7
  73.3 1.5 copy-start.9
  73.3 2.3 %copy-start.8 = (f32[384,3]{0,1:T(4,128)S(1)}, f32[384,3]{0,1:T(4,128)}, u32[]{:S(2)}) copy-start(f32[384,3]{0,1:T(4,128)} %constant.47.clone) | copy-start | bytes 13828
  94.2 5.8 %copy-start.1 = (f32[16,8,1728]{2,1,0:T(8,128)}, f32[16,8,1728]{2,1,0:T(8,128)S(1)}, u32[]{:S(2)}) copy-start(f32[16,8,1728]{2,1,0:T(8,128)S(1)} %all-to-all-done.blocks) | copy-start | bytes 2654212
  94.2 27.0 %all-to-all-start.3 = ((f32[16,8,1728]{2,1,0:T(8,128)}), f32[16,8,1728]{2,1,0:T(8,128)S(1)}, u32[]{:S(2)}, u32[]{:S(2)}) async-start(f32[16,8,1728]{2,1,0:T(8,128)} %shard_map.168), calls=%async_computation.3 | async-start | bytes 1835008 | tf_op jit(solution)/shard_map/all_to_all | solution.py:486
  121.2 4.8 %copy-start.3 = (f32[16,8,1728]{2,1,0:T(8,128)}, f32[16,8,1728]{2,1,0:T(8,128)S(1)}, u32[]{:S(2)}) copy-start(f32[16,8,1728]{2,1,0:T(8,128)S(1)} %all-to-all-done.3.blocks) | copy-start | bytes 2654212
  121.2 27.0 %all-to-all-start.1 = ((f32[16,8,1728]{2,1,0:T(8,128)}), f32[16,8,1728]{2,1,0:T(8,128)S(1)}, u32[]{:S(2)}, u32[]{:S(2)}) async-start(f32[16,8,1728]{2,1,0:T(8,128)} %shard_map.166), calls=%async_computation.1 | async-start | bytes 1835008 | tf_op jit(solution)/shard_map/all_to_all | solution.py:486
  148.2 0.9 copy-start

commit v2 on v1

--- a/solution.py
+++ b/solution.py
@@ -1,3 +1,4 @@
+import functools
 import math
 
 import jax
@@ -366,6 +367,65 @@
         out[:, lanes] = value if len(rest) == 1 else value + rest[0][:, lanes]
 
 
+def exchange_start(sent, received, send_sems, recv_sems, wait=False):
+    shards = sent.shape[0]
+    me = lax.axis_index("gx")
+
+    @pl.loop(1, shards)
+    def _(step):
+        peer = lax.rem(me + step, shards)
+        copy = pltpu.make_async_remote_copy(
+            src_ref=sent.at[peer],
+            dst_ref=received.at[me],
+            send_sem=send_sems.at[step],
+            recv_sem=recv_sems.at[step],
+            device_id={"gx": peer},
+            device_id_type=pl.DeviceIdType.MESH,
+        )
+        if wait:
+            copy.wait()
+        else:
+            copy.start()
+
+    if not wait:
+        received[me] = sent[me]
+
+
+def spectral_kernel(chunks, high, low, *refs):
+    tables = [refs[2 * c : 2 * c + 2] for c in range(chunks)]
+    constants = refs[2 * chunks : 2 * chunks + 8]
+    kappas = refs[2 * chunks + 8 : 3 * chunks + 8]
+    rates, out, sent, received, send_sems, recv_sems = refs[3 * chunks + 8 :]
+    shards = sent.shape[2]
+    me = lax.axis_index("gx")
+    barrier = pltpu.get_barrier_semaphore()
+
+    @pl.loop(1, shards)
+    def _(step):
+        pl.semaphore_signal(
+            barrier,
+            inc=1,
+            device_id={"gx": lax.rem(me + step, shards)},
+            device_id_type=pl.DeviceIdType.MESH,
+        )
+
+    def buffers(phase, c):
+        return (r.at[phase, c] for r in (sent, received, send_sems, recv_sems))
+
+    for c in range(chunks):
+        forward_kernel(high, low, *tables[c], sent.at[0, c])
+        if c == 0:
+            pl.semaphore_wait(barrier, shards - 1)
+        exchange_start(*buffers(0, c))
+    for c in range(chunks):
+        exchange_start(*buffers(0, c), wait=True)
+        solve_kernel(received.at[0, c], *constants, kappas[c], rates, sent.at[1, c])
+        exchange_start(*buffers(1, c))
+    for c in range(chunks):
+        exchange_start(*buffers(1, c), wait=True)
+        inverse_kernel(received.at[1, c], *tables[c], *((out, out) if c else (out,)))
+
+
 def call(kernel, shapes, flops, args, aliases=None):
     size = sum(math.prod(a.shape) * a.dtype.itemsize for a in (*args, *shapes))
     return pl.pallas_call(
@@ -469,9 +529,6 @@
     project = jnp.tile(mode_projection.T, (rows_here, rows_here))
     back = (eye[:, None, :, None] * vertical_modes.T[None, :, None, :]).reshape(lines, lines)
     rates = jnp.tile(mode_rates, rows_here)[None, :]
-    size = shards * CHUNK * 2
-    block = jax.ShapeDtypeStruct((shards, 8, PIECES * lines), F32)
-
     kappas, tables = [], []
     for c in range(chunks):
         wave = lax.axis_index("gx") * modes_here + c * CHUNK + jnp.arange(CHUNK, dtype=jnp.int32)
@@ -482,41 +539,29 @@
         )
         tables.append((jnp.asarray(t_high[c]), jnp.asarray(t_low[c])))
 
-    def swap(value):
-        return lax.all_to_all(value, "gx", split_axis=0, concat_axis=0, tiled=True)
-
-    received = []
-    for c in range(chunks):
-        (sent,) = call(
-            forward_kernel, [block], 6 * size * columns * lines, (high, low, *tables[c])
-        )
-        received.append(swap(sent))
-    returned = []
-    for c in range(chunks):
-        (solved,) = call(
-            solve_kernel,
-            [block],
-            12 * size * size * lines + 24 * size * lines * lines,
-            (
-                received[c],
-                *map(jnp.asarray, (*f_two, *g_two, twiddle_re, twiddle_im)),
-                project,
-                back,
-                kappas[c],
-                rates,
-            ),
-        )
-        returned.append(swap(solved))
-    total = ()
-    for c in range(chunks):
-        total = call(
-            inverse_kernel,
-            [jax.ShapeDtypeStruct((lines, columns), F32)],
-            6 * size * columns * lines,
-            (returned[c], *tables[c], *total),
-            {3: 0} if c else None,
-        )
-    return jnp.swapaxes(total[0].reshape(rows_here, levels, columns), 0, 1)
+    args = (
+        high,
+        low,
+        *(part for two in tables for part in two),
+        *map(jnp.asarray, (*f_two, *g_two, twiddle_re, twiddle_im)),
+        project,
+        back,
+        *kappas,
+        rates,
+    )
+    buffer = pltpu.VMEM((2, chunks, shards, 8, PIECES * lines), F32)
+    sems = pltpu.SemaphoreType.DMA((2, chunks, shards))
+    total = pl.pallas_call(
+        functools.partial(spectral_kernel, chunks),
+        out_shape=jax.ShapeDtypeStruct((lines, columns), F32),
+        in_specs=[pl.BlockSpec(memory_space=pltpu.VMEM)] * len(args),
+        out_specs=pl.BlockSpec(memory_space=pltpu.VMEM),
+        scratch_shapes=[buffer, buffer, sems, sems],
+        compiler_params=pltpu.CompilerParams(
+            collective_id=0, has_side_effects=True, vmem_limit_bytes=VMEM_BYTES
+        ),
+    )(*args)
+    return jnp.swapaxes(total.reshape(rows_here, levels, columns), 0, 1)
 
 
 def solution(mesh):

time: 157 us -> 131 us (0.83)
  waiting for transfers between devices: 58.2 us -> 11.7 us
  Pallas kernels: 68.8 us -> 106 us
  starting transfers between devices: 21.7 us -> 1.77 us
  local copies, waits for them, and re-layouts: 7.06 us -> 8.95 us
    pallas_call x0 -> x1, Pallas kernels: none -> 94.6 us  [body(): pl.pallas_call(functools.partial(spectral_kernel, chunks), out_shape=jax....]
    pallas_call x8 -> x2, Pallas kernels: 68.8 us -> 11.8 us  [call(): pl.pallas_call(kernel, out_shape=shapes, in_specs=[pl.BlockSpec(memory_sp...]
    all_to_all x4 -> x0, waiting for transfers between devices: 41.1 us -> none  [swap(): return lax.all_to_all(value, 'gx', split_axis=0, concat_axis=0, tiled=True)]
    all_to_all x4 -> x0, starting transfers between devices: 19.9 us -> none  [swap(): return lax.all_to_all(value, 'gx', split_axis=0, concat_axis=0, tiled=True)]
    ppermute x1, waiting for transfers between devices: 17.1 us -> 11.7 us  [body(): from_right = lax.ppermute(to_left, 'gx', [(j, i) for i, j in up])]
    unnamed x20 -> x13, local copies, waits for them, and re-layouts: 2.05 us -> 3.94 us
  transfers between devices with their start and end apart: 6 -> 2, of which waited for: 5 -> 1; matrix products, arithmetic and copies ran while one was open for 3% -> 4% of each run, Pallas kernels for 27% -> 0%
where the time goes in v2:
time: 131 us; the launch traced here: 129 us
  Pallas kernels  106 us (81%)
  waiting for transfers between devices  11.7 us (9%)
  local copies, waits for them, and re-layouts  8.95 us (7%)
  starting transfers between devices  1.77 us (1%)
    pallas_call x1, Pallas kernels, body(): pl.pallas_call(functools.partial(spectral_kernel, chunks), out_shape=jax....  94.6 us
    pallas_call x2, Pallas kernels, call(): pl.pallas_call(kernel, out_shape=shapes, in_specs=[pl.BlockSpec(memory_sp...  11.8 us
    ppermute x1, waiting for transfers between devices, body(): from_right = lax.ppermute(to_left, 'gx', [(j, i) for i, j in up])  11.7 us
    unnamed x13, local copies, waits for them, and re-layouts  3.94 us
  transfers between devices with their start and end apart: 2, of which 1 were waited for; matrix products, arithmetic and copies ran while one was open for 4% of the time, Pallas kernels for 0%

profile of v2, /device:TPU:13, one launch (start us, length us, event | category | flops | bytes accessed | tf_op | source)
XLA Modules:
  0.0 129.2 jit_solution(3380171464723413203)
XLA Ops:
  0.0 0.0 copy-start.4
  0.0 0.0 copy-start.2
  0.0 6.8 %shard_map.163 = (f32[6,48,1536]{2,1,0:T(8,128)}, f32[128,1536]{1,0:T(8,128)}, f32[96,1536]{1,0:T(8,128)}) custom-call(f32[6,48,1536]{2,1,0:T(8,128)} %bitcast.9, bf16[6,48,1536]{2,1,0:T(8,128)(2,1)} %bitcast.10), custom_call_target="tpu_custom_call" | custom-call | flops 17694720 | bytes 5799936 | tf_op jit(solution)/shard_map/pallas_call | solution.py:431
  6.9 0.0 copy-start.3
  6.9 1.8 %collective-permute-start = (f32[128,1536]{1,0:T(8,128)}, f32[128,1536]{1,0:T(8,128)S(1)}, u32[]{:S(2)}, u32[]{:S(2)}) collective-permute-start(f32[128,1536]{1,0:T(8,128)} %get-tuple-element.11), channel_id=1, source_target_pairs={{0,1},{1,2},{2,3},{3,4},{4,5},{5,6},{6,7},{7,8},{8,9},{9,10},{10,1... | collective-permute-start | bytes 2359304 | tf_op jit(solution)/shard_map/ppermute | solution.py:517
  8.6 0.0 collective-permute-start.1
  8.7 0.1 add.57
  8.8 0.1 add.51
  8.9 0.1 broadcast_in_dim_tile.12
  9.0 0.0 copy-done.4
  9.0 0.8 copy.27.refs_13_
  9.8 0.1 broadcast_in_dim_tile.11
  9.9 0.8 copy.26.refs_12_
  10.8 0.0 copy-done.2
  10.8 0.1 copy.25
  10.8 0.1 broadcast_multiply_fusion
  11.0 1.0 mul.28.refs_11_
  12.0 0.0 copy-start.5
  12.0 0.0 copy-done.3
  12.0 0.1 copy.24
  12.1 0.1 tile.14
  12.2 1.1 tile.15.refs_10_
  13.3 0.0 copy-done.5
  13.3 0.7 broadcast_in_dim_tile.13.refs_14_
  13.9 11.7 %collective-permute-done.1.after_in = f32[96,1536]{1,0:T(8,128)S(1)} collective-permute-done((f32[96,1536]{1,0:T(8,128)}, f32[96,1536]{1,0:T(8,128)S(1)}, u32[]{:S(2)}, u32[]{:S(2)}) %collective-permute-start.1) | collective-permute-done | bytes 589856 | tf_op jit(solution)/shard_map/ppermute | solution.py:518
  25.7 0.0 copy-start.1
  25.7 0.0 collective-permute-done.before_in
  25.7 0.8 copy-done.1
  26.5 0.2 copy-done
  26.8 5.0 %shard_map.164 = (bf16[288,1536]{1,0:T(8,128)(2,1)}, bf16[288,1536]{1,0:T(8,128)(2,1)}) custom-call(f32[6,48,1536]{2,1,0:T(8,128)} %get-tuple-element.10.interim, bf16[6,48,1536]{2,1,0:T(8,128)(2,1)} %bitcast.11, f32[128,1536]{1,0:T(8,128)} %copy-done, f32[96,1536]{1,0:T(8,128)} %copy-done.1), custom_call_target="tpu_custom_call" | custom-call | flops 17694720 | bytes 5799936 | tf_op jit(solution)/shard_map/pallas_call | solution.py:431
  31.7 94.6 %shard_map.165 = f32[288,1536]{1,0:T(8,128)} custom-call(bf16[288,1536]{1,0:T(8,128)(2,1)} %get-tuple-element.13.high, bf16[288,1536]{1,0:T(8,128)(2,1)} %get-tuple-element.14.low, bf16[768,1536]{1,0:T(8,128)(2,1)} %constant.48.clone.refs_0_, bf16[768,1536]{1,0:T(8,128)(2,1)} %constant.49.clone.refs_1_, bf16[768,1536]{1,0:T(8,128)(2,1)} %constant.50.clone.refs_2_, ...), custom_call_target="tpu_custom_call" | custom-call | tf_op jit(solution)/shard_map/pallas_call | solution.py:554
  126.3 2.9 %copy.29 = f32[48,6,1536]{2,0,1:T(8,128)} copy(f32[48,6,1536]{2,0,1:T(8,128)} %bitcast.8) | data formatting | bytes 3538944
  (12 shorter events, 0.1 us)
Async XLA Ops:
  0.0 9.0 %copy-start.4 = (f32[384,3]{0,1:T(4,128)S(1)}, f32[384,3]{0,1:T(4,128)}, u32[]{:S(2)}) copy-start(f32[384,3]{0,1:T(4,128)} %constant.47.clone) | copy-start | bytes 13828
  0.0 10.8 %copy-start.2 = (f32[48,48]{1,0:T(8,128)S(1)}, f32[48,48]{1,0:T(8,128)}, u32[]{:S(2)}) copy-start(f32[48,48]{1,0:T(8,128)} %param.20) | copy-start | bytes 27652
  6.9 5.2 %copy-start.3 = (f32[48,48]{1,0:T(8,128)S(1)}, f32[48,48]{1,0:T(8,128)}, u32[]{:S(2)}) copy-start(f32[48,48]{1,0:T(8,128)} %param.21) | copy-start | bytes 27652
  6.9 18.8 %collective-permute-start = (f32[128,1536]{1,0:T(8,128)}, f32[128,1536]{1,0:T(8,128)S(1)}, u32[]{:S(2)}, u32[]{:S(2)}) collective-permute-start(f32[128,1536]{1,0:T(8,128)} %get-tuple-element.11), channel_id=1, source_target_pairs={{0,1},{1,2},{2,3},{3,4},{4,5},{5,6},{6,7},{7,8},{8,9},{9,10},{10,1... | collective-permute-start | bytes 2359304 | tf_op jit(solution)/shard_map/ppermute | solution.py:517
  8.6 17.1 %collective-permute-start.1 = (f32[96,1536]{1,0:T(8,128)}, f32[96,1536]{1,0:T(8,128)S(1)}, u32[]{:S(2)}, u32[]{:S(2)}) collective-permute-start(f32[96,1536]{1,0:T(8,128)} %get-tuple-element.12), channel_id=1, source_target_pairs={{1,0},{2,1},{3,2},{4,3},{5,4},{6,5},{7,6},{8,7},{9,8},{10,9},{11,1... | collective-permute-start | bytes 1769480 | tf_op jit(solution)/shard_map/ppermute | solution.py:518
  12.0 1.2 copy-start.5
  25.7 0.8 copy-start.1
  25.7 1.1 copy-start

commit v3 on v2

--- a/solution.py
+++ b/solution.py
@@ -155,7 +155,7 @@
     return updated.reshape(levels, rows_here, columns)
 
 
-CHUNK = 24
+CHUNK = 16
 GROUP = 8
 SPAN = 2 * CHUNK
 PIECES = SPAN // 8

time: 131 us -> 126 us (0.962)
  Pallas kernels: 106 us -> 102 us
    pallas_call x1, Pallas kernels: 94.6 us -> 90.1 us  [body(): pl.pallas_call(functools.partial(spectral_kernel, chunks), out_shape=jax....]
    unnamed x13 -> x11, local copies, waits for them, and re-layouts: 3.94 us -> 3.77 us
  transfers between devices with their start and end apart: 2 -> 2, of which waited for: 1 -> 1; matrix products, arithmetic and copies ran while one was open for 4% -> 5% of each run, Pallas kernels for 0% -> 0%
where the time goes in v3:
time: 126 us; the launch traced here: 125 us
  Pallas kernels  102 us (81%)
  waiting for transfers between devices  10.9 us (9%)
  local copies, waits for them, and re-layouts  9.67 us (8%)
  starting transfers between devices  1.77 us (1%)
    pallas_call x1, Pallas kernels, body(): pl.pallas_call(functools.partial(spectral_kernel, chunks), out_shape=jax....  90.1 us
    pallas_call x2, Pallas kernels, call(): pl.pallas_call(kernel, out_shape=shapes, in_specs=[pl.BlockSpec(memory_sp...  11.8 us
    ppermute x1, waiting for transfers between devices, body(): from_right = lax.ppermute(to_left, 'gx', [(j, i) for i, j in up])  10.9 us
    unnamed x11, local copies, waits for them, and re-layouts  3.77 us
  transfers between devices with their start and end apart: 2, of which 1 were waited for; matrix products, arithmetic and copies ran while one was open for 5% of the time, Pallas kernels for 0%

profile of v3, /device:TPU:13, one launch (start us, length us, event | category | flops | bytes accessed | tf_op | source)
XLA Modules:
  0.0 124.7 jit_solution(1548344874739247741)
XLA Ops:
  0.0 0.0 copy-start.1
  0.0 6.8 %shard_map.181 = (f32[6,48,1536]{2,1,0:T(8,128)}, f32[128,1536]{1,0:T(8,128)}, f32[96,1536]{1,0:T(8,128)}) custom-call(f32[6,48,1536]{2,1,0:T(8,128)} %bitcast.9, bf16[6,48,1536]{2,1,0:T(8,128)(2,1)} %bitcast.10), custom_call_target="tpu_custom_call" | custom-call | flops 17694720 | bytes 5799936 | tf_op jit(solution)/shard_map/pallas_call | solution.py:431
  6.8 1.8 %collective-permute-start = (f32[128,1536]{1,0:T(8,128)}, f32[128,1536]{1,0:T(8,128)S(1)}, u32[]{:S(2)}, u32[]{:S(2)}) collective-permute-start(f32[128,1536]{1,0:T(8,128)} %get-tuple-element.11), channel_id=1, source_target_pairs={{0,1},{1,2},{2,3},{3,4},{4,5},{5,6},{6,7},{7,8},{8,9},{9,10},{10,1... | collective-permute-start | bytes 2359304 | tf_op jit(solution)/shard_map/ppermute | solution.py:517
  8.6 0.0 collective-permute-start.1
  8.6 0.0 copy-done.1
  8.6 0.1 copy.28
  8.7 0.1 broadcast_multiply_fusion
  8.9 0.0 copy-done.2
  8.9 0.1 copy.27
  9.0 0.1 tile.18
  9.1 0.0 copy-start.3
  9.1 0.0 copy-start.4
  9.1 1.1 tile.19.refs_12_
  10.2 1.0 mul.31.refs_13_
  11.2 0.1 broadcast_in_dim_tile.15
  11.3 0.1 add.89
  11.4 0.1 add.77
  11.4 0.1 add.83
  11.5 0.0 copy-done.3
  11.6 0.8 copy.29.refs_14_
  12.4 0.1 broadcast_in_dim_tile.16
  12.5 0.8 copy.30.refs_15_
  13.3 0.1 broadcast_in_dim_tile.17
  13.4 0.8 copy.31.refs_16_
  14.2 0.0 copy-done.4
  14.2 0.7 broadcast_in_dim_tile.18.refs_17_
  14.8 10.9 %collective-permute-done.1.after_in = f32[96,1536]{1,0:T(8,128)} collective-permute-done((f32[96,1536]{1,0:T(8,128)}, f32[96,1536]{1,0:T(8,128)}, u32[]{:S(2)}, u32[]{:S(2)}) %collective-permute-start.1) | collective-permute-done | bytes 589856 | tf_op jit(solution)/shard_map/ppermute | solution.py:518
  25.8 0.0 collective-permute-done.before_in
  25.8 0.9 copy-done
  26.7 5.0 %shard_map.182 = (bf16[288,1536]{1,0:T(8,128)(2,1)}, bf16[288,1536]{1,0:T(8,128)(2,1)}) custom-call(f32[6,48,1536]{2,1,0:T(8,128)} %get-tuple-element.10.interim, bf16[6,48,1536]{2,1,0:T(8,128)(2,1)} %bitcast.11, f32[128,1536]{1,0:T(8,128)} %copy-done, f32[96,1536]{1,0:T(8,128)} %collective-permute-done.1.after_in), custom_call_target="tpu_custom_call" | custom-call | flops 17694720 | bytes 5799936 | tf_op jit(solution)/shard_map/pallas_call | solution.py:431
  31.7 90.1 %shard_map.183 = f32[288,1536]{1,0:T(8,128)} custom-call(bf16[288,1536]{1,0:T(8,128)(2,1)} %get-tuple-element.13.high, bf16[288,1536]{1,0:T(8,128)(2,1)} %get-tuple-element.14.low, bf16[512,1536]{1,0:T(8,128)(2,1)} %constant.57.clone.refs_0_, bf16[512,1536]{1,0:T(8,128)(2,1)} %constant.58.clone.refs_1_, bf16[512,1536]{1,0:T(8,128)(2,1)} %constant.59.clone.refs_2_, ...), custom_call_target="tpu_custom_call" | custom-call | tf_op jit(solution)/shard_map/pallas_call | solution.py:554
  121.8 2.9 %copy.33 = f32[48,6,1536]{2,0,1:T(8,128)} copy(f32[48,6,1536]{2,0,1:T(8,128)} %bitcast.8) | data formatting | bytes 3538944
  (17 shorter events, 0.1 us)
Async XLA Ops:
  0.0 8.6 %copy-start.1 = (f32[48,48]{1,0:T(8,128)S(1)}, f32[48,48]{1,0:T(8,128)}, u32[]{:S(2)}) copy-start(f32[48,48]{1,0:T(8,128)} %param.22) | copy-start | bytes 27652
  0.0 8.9 %copy-start.2 = (f32[48,48]{1,0:T(8,128)S(1)}, f32[48,48]{1,0:T(8,128)}, u32[]{:S(2)}) copy-start(f32[48,48]{1,0:T(8,128)} %param.23) | copy-start | bytes 27652
  6.8 18.9 %collective-permute-start = (f32[128,1536]{1,0:T(8,128)}, f32[128,1536]{1,0:T(8,128)S(1)}, u32[]{:S(2)}, u32[]{:S(2)}) collective-permute-start(f32[128,1536]{1,0:T(8,128)} %get-tuple-element.11), channel_id=1, source_target_pairs={{0,1},{1,2},{2,3},{3,4},{4,5},{5,6},{6,7},{7,8},{8,9},{9,10},{10,1... | collective-permute-start | bytes 2359304 | tf_op jit(solution)/shard_map/ppermute | solution.py:517
  8.6 17.2 %collective-permute-start.1 = (f32[96,1536]{1,0:T(8,128)}, f32[96,1536]{1,0:T(8,128)}, u32[]{:S(2)}, u32[]{:S(2)}) collective-permute-start(f32[96,1536]{1,0:T(8,128)} %get-tuple-element.12), channel_id=1, source_target_pairs={{1,0},{2,1},{3,2},{4,3},{5,4},{6,5},{7,6},{8,7},{9,8},{10,9},{11,1... | collective-permute-start | bytes 1769480 | tf_op jit(solution)/shard_map/ppermute | solution.py:518
  9.1 2.5 %copy-start.3 = (f32[256,3]{0,1:T(4,128)S(1)}, f32[256,3]{0,1:T(4,128)}, u32[]{:S(2)}) copy-start(f32[256,3]{0,1:T(4,128)} %constant.56.clone) | copy-start | bytes 9220
  9.1 5.1 %copy-start.4 = (f32[48]{0:T(128)S(1)}, f32[48]{0:T(128)}, u32[]{:S(2)}) copy-start(f32[48]{0:T(128)} %param.24) | copy-start | bytes 580
  25.8 0.9 copy-start
